TPU v7x, 32 devices: a whole 2x2x4 slice. The times are simulated.
32 devices in a mesh: dp: 8 (over z, x), chan: 4 (over y, core).
Axes of the slice: x: 2, y: 2, z: 4, core: 2. Of those that a mesh axis runs over, the one named last changes fastest.
Arguments:
- tokens: bfloat16 [75264, 1024], P(('dp', 'chan')), may hold values from -6 to 6
- frame_counts: int32 [8], P('dp'), may hold values from 2 to 12, as said below
- cotangent: bfloat16 [75264, 1024], P(('dp', 'chan')), may hold values from -6 to 6
- w_reduce: float32 [2, 1024, 256], P(None, None, 'chan'), may hold values from -0.1875 to 0.1875
- w_mix: float32 [2, 256, 256], P(None, None, 'chan'), may hold values from -0.375 to 0.375
- w_depth: float32 [2, 27, 256], P(None, None, 'chan'), may hold values from -1.25 to 1.25
- w_expand: float32 [2, 256, 1024], P(None, 'chan'), may hold values from -0.375 to 0.375
- norm_mid: float32 [2, 3, 2, 256], P(None, None, None, 'chan'), may hold values from -1.2 to 1.4
- norm_out: float32 [2, 2, 1024], replicated, may hold values from -1.2 to 1.4
- moment_reduce: float32 [2, 1024, 256], P(None, None, 'chan'), may hold values from -2352 to 2352
- moment_mix: float32 [2, 256, 256], P(None, None, 'chan'), may hold values from -2352 to 2352
- moment_depth: float32 [2, 27, 256], P(None, None, 'chan'), may hold values from -2352 to 2352
- moment_expand: float32 [2, 256, 1024], P(None, 'chan'), may hold values from -2352 to 2352
- moment_mid: float32 [2, 3, 2, 256], P(None, None, None, 'chan'), may hold values from -2352 to 2352
- moment_out: float32 [2, 2, 1024], replicated, may hold values from -2352 to 2352
Outputs:
- output: bfloat16 [75264, 1024], P(('dp', 'chan'))
- grad_tokens: bfloat16 [75264, 1024], P(('dp', 'chan'))
- grad_reduce: float32 [2, 1024, 256], P(None, None, 'chan')
- grad_mix: float32 [2, 256, 256], P(None, None, 'chan')
- grad_depth: float32 [2, 27, 256], P(None, None, 'chan')
- grad_expand: float32 [2, 256, 1024], P(None, 'chan')
- grad_mid: float32 [2, 3, 2, 256], P(None, None, None, 'chan')
- grad_out: float32 [2, 2, 1024], replicated
- new_reduce: float32 [2, 1024, 256], P(None, None, 'chan')
- new_mix: float32 [2, 256, 256], P(None, None, 'chan')
- new_depth: float32 [2, 27, 256], P(None, None, 'chan')
- new_expand: float32 [2, 256, 1024], P(None, 'chan')
- new_mid: float32 [2, 3, 2, 256], P(None, None, None, 'chan')
- new_out: float32 [2, 2, 1024], replicated
- new_moment_reduce: float32 [2, 1024, 256], P(None, None, 'chan')
- new_moment_mix: float32 [2, 256, 256], P(None, None, 'chan')
- new_moment_depth: float32 [2, 27, 256], P(None, None, 'chan')
- new_moment_expand: float32 [2, 256, 1024], P(None, 'chan')
- new_moment_mid: float32 [2, 3, 2, 256], P(None, None, None, 'chan')
- new_moment_out: float32 [2, 2, 1024], replicated
Inputs may be any that keep to these rules, and one draw needn't show every extreme that they name: `frame_counts`: each clip has 2 to 12 real frames; some clip has exactly 12 and some exactly 2.
All inputs are finite; a program needn't handle non-finite values.
Results may differ from a plain program's by a relative error of at most 0.018.
Values may be sent and summed in bfloat16 or wider, within the bound.
A program may use at most 384 MiB of HBM per device.

v0:
```python
import functools

import jax
import jax.numpy as jnp
from jax import lax
from jax.experimental import pallas as pl
from jax.experimental.pallas import tpu as pltpu
from jax.sharding import PartitionSpec as P

FRAMES = 12
HH = 28
WW = 28
WP = 32
KVOL = 27
BLOCKS = 2
GROUP = 4
QUADS = HH // GROUP
FLAT = GROUP * WW
WIDE = GROUP * WP
PIECES = 8
TRIO = 3

EPS = 1e-05
LEARN_RATE = 0.001
MOMENTUM = 0.9
DECAY = 0.0001
MESH = pl.DeviceIdType.MESH
F32 = jnp.float32
BF16 = jnp.bfloat16
ROOT = 0.7978845608028654
CUBE = 0.044715


def gelu_core(v):
    square = v * v
    return square, jnp.tanh(v * (ROOT + (ROOT * CUBE) * square))


def gelu_value(v, t, half):
    h = half * v
    return h * t + h


def gelu_slope(v, square, t, half):
    r = v * (half * ROOT + (half * (3.0 * ROOT * CUBE)) * square)
    return (half * t + half) + (r - r * (t * t))


def dot_rows(left, right):
    return lax.dot_general(left, right, (((0,), (0,)), ((), ())), preferred_element_type=F32)


def dot(left, right):
    return jnp.dot(left, right, preferred_element_type=F32)


def fold(v):
    return jnp.sum(v.reshape(v.shape[0] // 8, 8, v.shape[1]), axis=0)


def spread(v):
    gap = jnp.zeros((WP - WW, v.shape[1]), v.dtype)
    parts = []
    for h in range(v.shape[0] // WW):
        parts += [v[WW * h : WW * (h + 1)], gap]
    return jnp.concatenate(parts, axis=0)


def squeeze(v):
    return jnp.concatenate([v[WP * h : WP * h + WW] for h in range(v.shape[0] // WP)], axis=0)


def pieces(v, rows):
    return [v[rows * k : rows * (k + 1)] for k in range(v.shape[0] // rows)]


def rows_of(*vectors):
    parts = []
    for v in vectors:
        parts += pieces_of(v)
    n = 4 if len(parts) <= 4 else 8
    out = []
    for side in range(2):
        out += [v[:, 128 * side : 128 * (side + 1)] for v in parts]
        if len(parts) < n:
            out.append(jnp.zeros((n - len(parts), 128), F32))
    return jnp.concatenate(out, axis=0)


def pieces_of(v):
    return [v[:, 256 * i : 256 * (i + 1)] for i in range(v.shape[1] // 256)]


def flat_sum(v):
    return jnp.sum(v, axis=0, keepdims=True)


def wide_row(v, first):
    return jnp.concatenate([v[first + i : first + i + 1] for i in range(4)], axis=1)


class Net:
    def __init__(self, groups, lanes):
        self.lanes = lanes
        self.low, self.high = stages(groups)
        self.row = lax.axis_index("dp")
        self.lane = lax.axis_index("chan")
        self.core = lax.rem(self.lane, 2)
        self.side = lax.div(self.lane, 2)
        self.half = lanes // 2
        self.row_low = lax.rem(self.row, self.low)
        self.row_high = lax.div(self.row, self.low)

    def near(self):
        return [(1 - self.core, (self.row, self.side * 2 + 1 - self.core))]

    def far(self):
        out = []
        for o in sorted(range(self.low), key=lambda o: abs(2 * o - self.low - 1)):
            for p in range(self.half):
                if o or p:
                    row = lax.rem(self.row_low + o, self.low)
                    side = lax.rem(self.side + p, self.half)
                    out.append((row * self.half + side, (self.row_high * self.low + row, side * 2 + self.core)))
        return out

    def far_slot(self):
        return self.row_low * self.half + self.side

    def top(self):
        rows = [lax.rem(self.row_high + o, self.high) for o in range(1, self.high)]
        return [(row, (row * self.low + self.row_low, self.lane)) for row in rows]

    def pair(self):
        lane = self.side * 2 + 1 - self.core
        return lane, (self.row, lane)

    def across(self):
        lane = (1 - self.side) * 2 + self.core
        return lane, (self.row, lane)

    def corner(self):
        return (1 - self.side) * 2 + 1 - self.core


def stages(groups):
    low = min(groups, 8)
    return low, groups // low


def push(src, dst, send, recv, device):
    copy = pltpu.make_async_remote_copy(
        src_ref=src, dst_ref=dst, send_sem=send, recv_sem=recv, device_id=device, device_id_type=MESH
    )
    return copy


def whole_kernel(
    groups,
    lanes,
    counts,
    tokens,
    cotangent,
    reduce_loc,
    mix_loc,
    expand_loc,
    small_loc,
    norm_out,
    out_hbm,
    gtok_hbm,
    grads_out,
    gmid_out,
    gout_out,
    x0,
    x1,
    yb,
    sb,
    red_t,
    exp,
    tbuf,
    mix_t,
    mix,
    small_in,
    small,
    z1,
    a1s,
    z2,
    dz,
    hz,
    conv,
    a3s,
    edge,
    pat,
    d2s,
    halo_send,
    halo_recv,
    grad_a,
    grad_ra,
    grad_b,
    grad_rb,
    grad_all,
    grad_top,
    near,
    far,
    top,
    near_send,
    near_recv,
    far_send,
    far_recv,
    top_send,
    top_recv,
    gather_send,
    gather_recv,
    halo_ssem,
    halo_rsem,
    load_sem,
    store_sem,
    grad_sa,
    grad_qa,
    grad_sb,
    grad_qb,
    grad_sc,
    grad_qc,
    grad_st,
    grad_qt,
    weight_sem,
):
    net = Net(groups, lanes)
    lane = net.lane
    frames = tokens.shape[0] // (HH * WW)
    frame_rows = HH * WW
    last = frames - 1
    count_here = counts[0]
    xs = (x0, x1)

    def live(frame):
        position = lane * frames + frame
        return jnp.where((position >= 0) & (position < count_here), 1.0, 0.0)

    def frame_copy(src, dst, f, sem):
        rows = pl.ds(f * frame_rows, frame_rows)
        return pltpu.make_async_copy(src.at[rows], dst.at[rows], sem)

    loads = [frame_copy(tokens, x0, f, load_sem.at[f]) for f in range(frames)]
    cot_load = pltpu.make_async_copy(cotangent, sb, load_sem.at[frames])
    for copy in loads:
        copy.start()
    cot_load.start()
    weight_loads = {}
    for b in range(BLOCKS):
        places = [
            ("red", reduce_loc.at[b], grads_out.at[b, pl.ds(0, 64)]),
            ("exp", expand_loc.at[b], grads_out.at[b, pl.ds(64, 64)]),
            ("mix", mix_loc.at[b, pl.ds(0, 32)], grads_out.at[b, pl.ds(128, 32), pl.ds(0, 256)]),
            ("mix", mix_loc.at[b, pl.ds(32, 32)], grads_out.at[b, pl.ds(128, 32), pl.ds(256, 256)]),
        ]
        for k, (name, src, dst) in enumerate(places):
            copy = pltpu.make_async_copy(src, dst, weight_sem.at[b, k])
            copy.start()
            weight_loads.setdefault((name, b), []).append(copy)

    barrier = pltpu.get_barrier_semaphore()
    friends = [d for peers in (net.near(), net.far(), net.top()) for _, d in peers] + [(net.row, net.corner())]
    for device in friends:
        pl.semaphore_signal(barrier, inc=1, device_id=device, device_id_type=MESH)
    pl.semaphore_wait(barrier, len(friends))

    own = net.lane
    share = red_t.shape[1] // lanes
    late = []

    def gather(name, b):
        slot, dst_of = plan[name, b]
        mine = dst_of(own)
        for copy in weight_loads.get((name, b), []):
            copy.wait()
        if name == "red":
            mine[...] = grads_out[b, :64].astype(BF16)
        elif name == "exp":
            mine[...] = grads_out[b, 64:128].astype(BF16)
        elif name == "mix":
            parts = [grads_out[b, 128:160, :256], grads_out[b, 128:160, 256:512]]
            mine[...] = jnp.concatenate(parts, axis=0).astype(BF16)
        else:
            mine[...] = small_loc[...]
        for step, (_, device) in enumerate((net.pair(), net.across())):
            copy = push(mine, mine, gather_send.at[slot, step], gather_recv.at[slot, own], device)
            copy.start()
            late.append(copy)

    def gather_on(name, b):
        slot, dst_of = plan[name, b]
        who, device = net.across()
        piece = dst_of(who)
        push(piece, piece, gather_send.at[slot, 1], gather_recv.at[slot, who], device).wait_recv()
        copy = push(piece, piece, gather_send.at[slot, 2], gather_recv.at[slot, who], net.pair()[1])
        copy.start()
        late.append(copy)

    def gather_wait(name, b):
        slot, dst_of = plan[name, b]
        for who in (net.pair()[0], net.corner()):
            push(dst_of(who), dst_of(who), gather_send.at[slot, 0], gather_recv.at[slot, who], net.pair()[1]).wait_recv()

    def block_rows(ref, b):
        return lambda who: ref.at[b, pl.ds(pl.multiple_of(who * share, share), share)]

    plan = {
        ("red", 0): (0, block_rows(red_t, 0)),
        ("mix", 0): (1, block_rows(mix_t, 0)),
        ("small", 0): (2, lambda who: small_in.at[who]),
        ("exp", 0): (3, block_rows(exp, 0)),
        ("red", 1): (4, block_rows(red_t, 1)),
        ("mix", 1): (5, block_rows(mix_t, 1)),
        ("exp", 1): (6, block_rows(exp, 1)),
    }
    for name in (("red", 0), ("mix", 0), ("small", 0)):
        gather(*name)

    used = {}
    travelling = []

    def total_start(i, value):
        size = value.shape[0]
        used[i] = size
        turn = i % 2
        gone, travelling[:] = list(travelling), []
        near[turn, net.core, :size] = value
        for who, device in net.near():
            mine = near.at[turn, net.core, pl.ds(0, size)]
            copy = push(mine, mine, near_send.at[i], near_recv.at[i], device)
            copy.start()
            travelling.append(copy)
            copy.wait_recv()
        far[turn, net.far_slot(), :size] = near[turn, 0, :size] + near[turn, 1, :size]
        for step, (who, device) in enumerate(net.far()):
            mine = far.at[turn, net.far_slot(), pl.ds(0, size)]
            copy = push(mine, mine, far_send.at[i, step], far_recv.at[i, net.far_slot()], device)
            copy.start()
            travelling.append(copy)
        for copy in gone:
            copy.wait_send()

    def total_finish(i):
        size = used[i]
        turn = i % 2
        for step, (who, device) in enumerate(net.far()):
            there = far.at[turn, who, pl.ds(0, size)]
            push(there, there, far_send.at[i, step], far_recv.at[i, who], device).wait_recv()
        total = far[turn, 0, :size]
        for j in range(1, net.low * net.half):
            total = total + far[turn, j, :size]
        if net.high > 1:
            mine = top.at[turn, net.row_high, pl.ds(0, size)]
            top[turn, net.row_high, :size] = total
            for step, (who, device) in enumerate(net.top()):
                copy = push(mine, mine, top_send.at[i, step], top_recv.at[i, net.row_high], device)
                copy.start()
                travelling.append(copy)
            for step, (who, device) in enumerate(net.top()):
                there = top.at[turn, who, pl.ds(0, size)]
                push(there, there, top_send.at[i, step], top_recv.at[i, who], device).wait_recv()
            total = top[turn, 0, :size]
            for j in range(1, net.high):
                total = total + top[turn, j, :size]
        return jnp.concatenate([total[: size // 2], total[size // 2 :]], axis=1)

    def halo_copy(kind, slot, side):
        step = -1 if side == 0 else 1
        return push(
            halo_send.at[side],
            halo_recv.at[slot, 1 - side],
            halo_ssem.at[kind, side],
            halo_rsem.at[kind, 1 - side],
            (net.row, lane + step),
        )

    def sends_to(side):
        return lane > 0 if side == 0 else lane < lanes - 1

    def halo_start(kind, slot, side):
        @pl.when(sends_to(side))
        def _():
            halo_copy(kind, slot, side).start()

    def halo_sent(kind, slot, side):
        @pl.when(sends_to(side))
        def _():
            halo_copy(kind, slot, side).wait_send()

    def halo_wait(kind, slot, side):
        step = -1 if side == 0 else 1
        push(
            halo_send.at[1 - side],
            halo_recv.at[slot, side],
            halo_ssem.at[kind, 1 - side],
            halo_rsem.at[kind, side],
            (net.row, lane + step),
        ).wait_recv()

    column = lax.broadcasted_iota(jnp.int32, (WIDE, 256), 0) % WP
    pad_mask = (column < WW).astype(F32)

    def half_mask(alive, lines):
        return jnp.concatenate([pad_mask[:WP] * (0.5 * alive)] * lines, axis=0)

    def affine(total, square, count, gain, shift):
        mean = total / count
        var = square / count - mean * mean
        scale = lax.rsqrt(var + EPS)
        return mean, scale, gain * scale, shift - mean * (gain * scale)

    def back_affine(e_sum, ez_sum, count, norm):
        mean, scale, a, _ = norm
        gain_grad = scale * (ez_sum - mean * e_sum)
        slope = -a * scale * gain_grad / count
        bias = -a * e_sum / count - slope * mean
        return slope, bias, gain_grad, e_sum

    def zero8(n=256):
        return jnp.zeros((8, n), F32)

    blank = jnp.zeros((WP, 256), F32)
    for f in range(frames):
        for b in range(BLOCKS):
            z2[b, f, 0] = blank
            z2[b, f, HH + 1] = blank
        dz[f, 0] = blank
        dz[f, HH + 1] = blank
    for side in range(2):
        hz[side, 0] = blank
        hz[side, HH + 1] = blank

    for name in (("red", 0), ("mix", 0), ("small", 0)):
        gather_on(*name)
    gather_wait("red", 0)
    tbuf[...] = red_t[0].T

    carry = (zero8(), zero8())
    for f in range(frames):
        loads[f].wait()
        alive = live(f)

        z = dot(x0[f * frame_rows : (f + 1) * frame_rows], tbuf[...])
        z1[0, f * HH : (f + 1) * HH] = spread(z).reshape(HH, WP, 256)
        carry = (carry[0] + fold(z) * alive, carry[1] + fold(z * z) * alive)

    alive_all = sum(live(f) for f in range(frames)) * (HH * WW)
    here_count = jnp.full((1, 256), 1.0, F32) * alive_all
    total_start(0, rows_of(flat_sum(carry[0]), flat_sum(carry[1]), here_count))

    gather_wait("small", 0)
    half_rows = small_loc.shape[0]
    for side in range(2):
        here = [small_in[who, :, 64 * side : 64 * (side + 1)] for who in range(lanes)]
        small[half_rows * side : half_rows * (side + 1)] = jnp.concatenate(here, axis=1)

    def mid(b, norm, which):
        r = BLOCKS * KVOL + (b * 3 + norm) * 2 + which
        return small[r : r + 1]

    edge_sums = []
    pattern_col = lax.broadcasted_iota(jnp.int32, (WP, 256), 0)
    for b in range(BLOCKS):
        taps_b = [[small[b * KVOL + dt * 9 + k : b * KVOL + dt * 9 + k + 1] for k in range(9)] for dt in range(3)]
        se = jnp.zeros((1, 256), F32)
        see = jnp.zeros((1, 256), F32)
        for f in range(-1, frames + 1):
            here = live(f)
            t = [
                here * (live(f - 1) * taps_b[0][k] + here * taps_b[1][k] + live(f + 1) * taps_b[2][k])
                for k in range(9)
            ]
            for cls in range(3):
                use = [dh for dh in range(3) if not (cls == 0 and dh == 0) and not (cls == 2 and dh == 2)]
                col = []
                for dw in range(3):
                    v = t[use[0] * 3 + dw]
                    for dh in use[1:]:
                        v = v + t[dh * 3 + dw]
                    col.append(v)
                inner = col[0] + col[1] + col[2]
                left, right = col[1] + col[2], col[0] + col[1]
                edge[b, f + 1, cls] = jnp.where(
                    pattern_col == 0,
                    left,
                    jnp.where(pattern_col == WW - 1, right, jnp.where(pattern_col < WW - 1, inner, 0.0)),
                )
                if 0 <= f < frames:
                    times = 1.0 if cls != 1 else HH - 2.0
                    se = se + times * (left + right + (WW - 2.0) * inner)
                    see = see + times * (left * left + right * right + (WW - 2.0) * (inner * inner))
        edge_sums.append((se, see))

    gather_wait("mix", 0)
    mix[...] = mix_t[0].T

    got = total_finish(0)
    count = got[2:3]
    count4 = jnp.concatenate([count] * 4, axis=1)
    first_sums = (got[0:1], got[1:2])

    def edge_rows(ref, j):
        top = jnp.where(j == 0, 0, 1)
        bottom = jnp.where(j == QUADS - 1, 2, 1)
        middle = ref[1]
        return jnp.concatenate([ref[top], middle, middle, ref[bottom]], axis=0)

    def trio(i):
        rows = pl.ds(pl.multiple_of(i * (TRIO * FLAT), TRIO * FLAT), TRIO * FLAT)
        lines = pl.ds(i * (TRIO * GROUP), TRIO * GROUP)
        where = []
        for k in range(TRIO):
            q = TRIO * i + k
            where.append((lax.div(q, QUADS), lax.rem(q, QUADS)))
        return rows, lines, where

    trios = frames * QUADS // TRIO

    def norm3_pattern(b, a3, b2, b3):
        for f in range(frames):
            for cls in range(3):
                pat[f + 1, cls] = edge[b, f + 1, cls] * (a3 * b2) + b3

    def row_class(h):
        return jnp.where(h == 0, 0, jnp.where(h == HH - 1, 2, 1))

    def convolve(local, f, b, flip, emit, acc):
        done = []
        for half in range(2):
            cols = slice(128 * half, 128 * (half + 1))
            kern = [small[b * KVOL + k : b * KVOL + k + 1, cols] for k in range(KVOL)]
            if flip:
                kern = kern[::-1]
            planes = []
            for dt in range(3):
                g = f + dt - 1
                planes.append(hz.at[0] if g < 0 else hz.at[1] if g > last else local.at[g])

            def two_rows(i, carry):
                h = 2 * i
                part = [[None] * 3 for _ in range(2)]
                for dt in range(3):
                    for rr in range(4):
                        v = planes[dt][h + rr, :, cols]
                        for o in range(2):
                            dh = rr - o
                            if 0 <= dh < 3:
                                for dw in range(3):
                                    term = kern[dt * 9 + dh * 3 + dw] * v
                                    part[o][dw] = term if part[o][dw] is None else part[o][dw] + term
                for o in range(2):
                    p = part[o]
                    c = p[1] + pltpu.roll(p[0], 1, 0) + pltpu.roll(p[2], WP - 1, 0)
                    carry = emit(h + o, half, cols, c, carry)
                return carry

            done.append(lax.fori_loop(0, HH // 2, two_rows, tuple(a[half] for a in acc)))
        return [[done[0][k], done[1][k]] for k in range(len(acc))]

    class Reduction:
        def __init__(self, first, size):
            self.lines = pl.ds(first, size)
            self.first, self.size = first, size
            self.which = 0 if first == 0 else 1
            self.open = {"a": [], "b": [], "all": []}

        def put(self, who, piece, first, value):
            grad_a[who, piece, pl.ds(self.lines.start + first, value.shape[0])] = value.astype(BF16)

        def clear(self, *names):
            for name in names:
                for copy in self.open[name]:
                    copy.wait_send()
                self.open[name] = []

        def move(self, name, copy):
            copy.start()
            self.open[name].append(copy)

        def pair_copy(self, b, side):
            i = 2 * b + self.which
            src, dst = grad_a.at[2 * side + 1 - net.core, :, self.lines], grad_ra.at[side, :, self.lines]
            return push(src, dst, grad_sa.at[i, side], grad_qa.at[i, side], net.pair()[1])

        def to_pair(self, b):
            for side in range(2):
                self.move("a", self.pair_copy(b, side))

        def across_copy(self, b):
            i = 2 * b + self.which
            src, dst = grad_a.at[net.across()[0], :, self.lines], grad_ra.at[2, :, self.lines]
            return push(src, dst, grad_sa.at[i, 2], grad_qa.at[i, 2], net.across()[1])

        def to_side(self, b):
            for side in range(2):
                self.pair_copy(b, side).wait_recv()
            other = net.across()[0]

            def add(piece, _):
                mine, theirs = grad_a[other, piece, self.lines], grad_ra[1 - net.side, piece, self.lines]
                grad_a[other, piece, self.lines] = (mine.astype(F32) + theirs.astype(F32)).astype(BF16)
                return 0

            lax.fori_loop(0, PIECES, add, 0)
            self.move("a", self.across_copy(b))

        def low_peers(self):
            rows = [lax.rem(net.row_low + o, net.low) for o in range(1, net.low)]
            return [(row, (net.row_high * net.low + row, lane)) for row in rows]

        def to_rows(self, b):
            i = 2 * b + self.which
            self.across_copy(b).wait_recv()
            self.clear("b")

            def add(piece, _):
                total = grad_a[own, piece, self.lines].astype(F32) + grad_ra[net.side, piece, self.lines].astype(F32)
                grad_b[piece, self.lines] = (total + grad_ra[2, piece, self.lines].astype(F32)).astype(BF16)
                return 0

            lax.fori_loop(0, PIECES, add, 0)
            each = PIECES // net.low
            for step, (who, device) in enumerate(self.low_peers()):
                src = grad_b.at[pl.ds(who * each, each), self.lines]
                dst = grad_rb.at[net.row_low, :, self.lines]
                self.move("b", push(src, dst, grad_sb.at[i, step], grad_qb.at[i, net.row_low], device))

        def to_all(self, b):
            i = 2 * b + self.which
            each = PIECES // net.low
            mine = pl.ds(net.row_low * each, each)
            for step, (who, device) in enumerate(self.low_peers()):
                src, dst = grad_b.at[mine, self.lines], grad_rb.at[who, :, self.lines]
                push(src, dst, grad_sb.at[i, step], grad_qb.at[i, who], device).wait_recv()
            total = grad_b[mine, self.lines].astype(F32)
            for who, _device in self.low_peers():
                total = total + grad_rb[who, :, self.lines].astype(F32)
            if net.high > 1:
                grad_top[b, net.row_high, :, self.lines] = total.astype(BF16)
                for step, (who, device) in enumerate(net.top()):
                    here = grad_top.at[b, net.row_high, :, self.lines]
                    self.move("all", push(here, here, grad_st.at[i, step], grad_qt.at[i, net.row_high], device))
                for step, (who, device) in enumerate(net.top()):
                    there = grad_top.at[b, who, :, self.lines]
                    push(there, there, grad_st.at[i, step], grad_qt.at[i, who], device).wait_recv()
                self.clear("all")
                total = grad_top[b, 0, :, self.lines].astype(F32)
                for j in range(1, net.high):
                    total = total + grad_top[b, j, :, self.lines].astype(F32)
            self.clear("all")
            grad_all[mine, self.lines] = total.astype(BF16)
            for step, (who, device) in enumerate(self.low_peers()):
                here = grad_all.at[mine, self.lines]
                self.move("all", push(here, here, grad_sc.at[i, step], grad_qc.at[i, net.row_low], device))

        def finish(self, b):
            i = 2 * b + self.which
            each = PIECES // net.low
            for step, (who, device) in enumerate(self.low_peers()):
                there = grad_all.at[pl.ds(who * each, each), self.lines]
                push(there, there, grad_sc.at[i, step], grad_qc.at[i, who], device).wait_recv()
            for piece in range(PIECES):
                cols = slice(128 * piece, 128 * (piece + 1))
                grads_out[b, self.first : self.first + self.size, cols] = grad_all[piece, self.lines].astype(F32)

    early = [Reduction(0, 96 if b == 0 else 80) for b in range(BLOCKS)]
    final = [Reduction(96, 64 if b == 0 else 80) for b in range(BLOCKS)]

    order = (0, last) + tuple(range(1, last))
    norms = []
    mid_grads = {}
    out_grads = {}

    def open_block(b, rows):
        z = dot(a3s[b, rows], exp[b])
        a4, b4 = norms[b][3][2], norms[b][3][3]
        return z, (z * a4 + b4) + xs[b][rows].astype(F32)

    out_store = [frame_copy(yb, out_hbm, f, store_sem.at[f]) for f in range(frames)]

    for b in range(BLOCKS):
        norm1 = affine(first_sums[0], first_sums[1], count, mid(b, 0, 0), mid(b, 0, 1))
        if b == 0:
            gather("exp", 0)
        _, _, a1, b1 = norm1
        carry = (zero8(), zero8())
        if b > 0:
            for side in range(2):
                halo_sent(2 * (b - 1) + 1, 2 + b - 1, side)
        for f in order:
            alive = live(f)

            v = z1[b, f * HH : (f + 1) * HH].reshape(HH * WP, 256) * a1 + b1
            _, t = gelu_core(v)
            m = dot(gelu_value(v, t, half_mask(alive, HH)).astype(BF16), mix[...])
            z2[b, f, 1 : 1 + HH] = m.reshape(HH, WP, 256)
            if f in (0, last):
                halo_send[0 if f == 0 else 1] = m.astype(BF16).reshape(HH, WP, 256)
            carry = (carry[0] + fold(m), carry[1] + fold(m * m))
            if f in (0, last):
                halo_start(2 * b, b, 0 if f == 0 else 1)

        def emit_conv(f):
            pad = pad_mask[:WP, :128] * live(f)

            def emit(row, half, cols, c, carry):
                c = c * pad
                conv[b, f * HH + row, :, cols] = c
                if f in (0, last):
                    halo_send[0 if f == 0 else 1, row, :, cols] = c.astype(BF16)
                e = edge[b, f + 1, row_class(row), :, cols]
                s0, s1, s2 = carry
                return (s0 + fold(c), s1 + fold(c * c), s2 + fold(c * e))

            return emit

        def fill(side):
            present = lane > 0 if side == 0 else lane < lanes - 1

            @pl.when(present)
            def _():
                halo_wait(2 * b, b, side)

                def widen(j, _):
                    hz[side, pl.ds(1 + j * GROUP, GROUP)] = halo_recv[b, side, pl.ds(j * GROUP, GROUP)].astype(F32)
                    return 0

                lax.fori_loop(0, QUADS, widen, 0)

            @pl.when(jnp.logical_not(present))
            def _():
                def clear(j, _):
                    hz[side, pl.ds(1 + j * GROUP, GROUP)] = jnp.zeros((GROUP, WP, 256), F32)
                    return 0

                lax.fori_loop(0, QUADS, clear, 0)

        acc = [[zero8(128), zero8(128)] for _ in range(3)]
        for f in range(1, last):
            acc = convolve(z2.at[b], f, b, False, emit_conv(f), acc)
        if b == 0:
            gather_on("exp", 0)
        for side in range(2):
            fill(side)
            halo_sent(2 * b, b, side)
            f = 0 if side == 0 else last
            acc = convolve(z2.at[b], f, b, False, emit_conv(f), acc)
            halo_start(2 * b + 1, 2 + b, side)
        joined = [jnp.concatenate([flat_sum(a[0]), flat_sum(a[1])], axis=1) for a in acc]
        total_start(3 * b + 1, rows_of(flat_sum(carry[0]), flat_sum(carry[1]), *joined, *edge_sums[b]))
        if b == 0:
            gather_wait("exp", 0)
        else:
            gather_wait("exp", 1)
            tbuf[...] = exp[1].T
        got = total_finish(3 * b + 1)
        norm2 = affine(got[0:1], got[1:2], count, mid(b, 1, 0), mid(b, 1, 1))
        _, _, a2, b2 = norm2
        sc, scc, sce, se, see = [got[i : i + 1] for i in range(2, 7)]
        total3 = a2 * sc + b2 * se
        square3 = a2 * a2 * scc + 2.0 * a2 * b2 * sce + b2 * b2 * see
        norm3 = affine(total3, square3, count, mid(b, 2, 0), mid(b, 2, 1))
        _, _, a3, b3 = norm3

        norm3_pattern(b, a3, b2, b3)
        if b == 0:
            gather("red", 1)
            gather("mix", 1)

        def activate(i, _):
            rows, lines, where = trio(i)
            c = conv[b, lines].reshape(TRIO * WIDE, 256)
            acts = []
            for k, (f, j) in enumerate(where):
                v = c[WIDE * k : WIDE * (k + 1)] * (a3 * a2) + edge_rows(pat.at[f + 1], j)
                _, t = gelu_core(v)
                acts.append(squeeze(gelu_value(v, t, 0.5 * live(f))))
            a3s[b, rows] = jnp.concatenate(acts, axis=0).astype(BF16)
            return 0

        lax.fori_loop(0, trios, activate, 0)
        gram = dot_rows(a3s[b], a3s[b])
        line = dot(jnp.ones((16, frames * frame_rows), BF16), a3s[b])
        high = jnp.concatenate([gram, line], axis=0)
        split = high.astype(BF16)
        grown = dot(split, exp[b]) + dot((high - split.astype(F32)).astype(BF16), exp[b])
        squares = flat_sum(fold(grown[:256] * exp[b].astype(F32)))
        if b == 0:
            gather_on("red", 1)
            gather_on("mix", 1)
        total_start(3 * b + 2, rows_of(grown[256:257], squares))
        if b == 0:
            gather_wait("red", 1)
            tbuf[...] = red_t[1].T
        got = total_finish(3 * b + 2)
        norm4 = affine(wide_row(got, 0), wide_row(got, 4), count4, norm_out[b, 0:1], norm_out[b, 1:2])
        norms.append((norm1, norm2, norm3, norm4, (sc, scc, sce, se, see)))

        if b == 0:
            gather("exp", 1)

            def closing(i, carry):
                rows, lines, where = trio(i)
                _, pre = open_block(0, rows)
                results = []
                for (f, j), v in zip(where, pieces(pre, FLAT)):
                    _, t = gelu_core(v)
                    results.append(gelu_value(v, t, 0.5 * live(f)).astype(BF16))
                result = jnp.concatenate(results, axis=0)
                x1[rows] = result
                z = dot(result, tbuf[...])
                z1[1, lines] = spread(z).reshape(TRIO * GROUP, WP, 256)
                return (carry[0] + fold(z), carry[1] + fold(z * z))

            carry = lax.fori_loop(0, trios, closing, (zero8(), zero8()))
            gather_on("exp", 1)
            total_start(3, rows_of(flat_sum(carry[0]), flat_sum(carry[1])))
            gather_wait("mix", 1)
            mix[...] = mix_t[1].T
            got = total_finish(3)
            first_sums = (got[0:1], got[1:2])

    cot_load.wait()

    def ending(i, carry):
        rows, lines, where = trio(i)
        z, pre = open_block(1, rows)
        g = sb[rows]
        s0, s1 = carry
        for k, (f, j) in enumerate(where):
            here = slice(FLAT * k, FLAT * (k + 1))
            v, half = pre[here], 0.5 * live(f)
            square, t = gelu_core(v)
            part = pl.ds(pl.multiple_of((TRIO * i + k) * FLAT, FLAT), FLAT)
            yb[part] = gelu_value(v, t, half).astype(BF16)
            s = gelu_slope(v, square, t, half) * g[here].astype(F32)
            sb[part] = s.astype(BF16)
            s0, s1 = s0 + fold(s), s1 + fold(s * z[here])
        return s0, s1

    carry = lax.fori_loop(0, trios, ending, (zero8(1024), zero8(1024)))
    total_start(6, rows_of(flat_sum(carry[0]), flat_sum(carry[1])))
    for copy in out_store:
        copy.start()

    for b in reversed(range(BLOCKS)):
        turn = BLOCKS - 1 - b
        base = 6 + 3 * turn
        norm1, norm2, norm3, norm4, (sc, scc, sce, se, see) = norms[b]
        _, _, a1, b1 = norm1
        mean2, scale2, a2, b2 = norm2
        mean3, scale3, a3, b3 = norm3
        a4 = norm4[2]

        got = total_finish(base)
        slope4, bias4, gain_grad, shift_grad = back_affine(wide_row(got, 0), wide_row(got, 4), count4, norm4)
        out_grads[b] = (gain_grad, shift_grad)
        if turn == 0:
            for copy in out_store:
                copy.wait()
        for side in range(2):
            if turn == 0:
                halo_sent(2 * (BLOCKS - 1) + 1, 2 + BLOCKS - 1, side)
            else:
                halo_sent(2 * BLOCKS + turn - 1, b + 1, side)

        if turn > 0:
            early[b + 1].to_rows(b + 1)
            final[b + 1].to_side(b + 1)
        kind = 2 * BLOCKS + turn
        norm3_pattern(b, a3, b2, b3)
        acc = (zero8(), zero8(), zero8())
        for f in order:
            alive = live(f)

            rows = slice(f * frame_rows, (f + 1) * frame_rows)
            z = dot(a3s[b, rows], exp[b])
            d4 = (sb[rows].astype(F32) * a4 + (z * slope4 + bias4 * alive)).astype(BF16)
            yb[rows] = d4
            back = spread(dot(d4, tbuf[...]))
            for j in range(QUADS):
                c = conv[b, f * HH + GROUP * j : f * HH + GROUP * (j + 1)].reshape(WIDE, 256)
                v = c * (a3 * a2) + edge_rows(pat.at[f + 1], j)
                square, t = gelu_core(v)
                e3 = back[WIDE * j : WIDE * (j + 1)] * gelu_slope(v, square, t, 0.5)
                dz[f, 1 + GROUP * j : 1 + GROUP * (j + 1)] = e3.reshape(GROUP, WP, 256)
                if f in (0, last):
                    halo_send[0 if f == 0 else 1, GROUP * j : GROUP * (j + 1)] = e3.astype(BF16).reshape(GROUP, WP, 256)
                e = edge_rows(edge.at[b, f + 1], j)
                acc = (acc[0] + fold(e3), acc[1] + fold(e3 * c), acc[2] + fold(e3 * e))
            if f in (0, last):
                halo_start(kind, b, 0 if f == 0 else 1)
        total_start(base + 1, rows_of(*[flat_sum(a) for a in acc]))

        if turn > 0:
            early[b + 1].clear("a")

        def expand_grad(i, _):
            cols = pl.ds(pl.multiple_of(i * 256, 256), 256)
            g = dot_rows(a3s[b], yb[:, cols])
            for who in range(lanes):
                for h in range(2):
                    early[b].put(who, 2 * i + h, 0, g[share * who : share * (who + 1), 128 * h : 128 * (h + 1)])
            return 0

        lax.fori_loop(0, 4, expand_grad, 0)
        if b > 0:
            tbuf[...] = exp[b - 1].T

        got = total_finish(base + 1)
        e3_sum, e3_conv, e3_edge = got[0:1], got[1:2], got[2:3]
        e3_third = a2 * e3_conv + b2 * e3_edge
        slope3, bias3, gain3, shift3 = back_affine(e3_sum, e3_third, count, norm3)
        third_conv = a2 * scc + b2 * sce
        third_edge = a2 * sce + b2 * see
        d3_conv = a3 * e3_conv + bias3 * sc + slope3 * third_conv
        d3_edge = a3 * e3_edge + bias3 * se + slope3 * third_edge
        slope2, bias2, gain2, shift2 = back_affine(d3_edge, d3_conv, count, norm2)

        if turn > 0:
            early[b + 1].to_all(b + 1)
            final[b + 1].to_rows(b + 1)
        for f in range(-1, frames + 1):
            live_pad = pad_mask[:WP] * live(f)
            for cls in range(3):
                pat[f + 1, cls] = bias3 * live_pad + (slope3 * b2) * edge[b, f + 1, cls]
        slope_c = slope3 * a2

        def to_d3(q, _):
            f = lax.div(q, QUADS)
            j = lax.rem(q, QUADS)
            rows = pl.ds(1 + j * GROUP, GROUP)
            c = conv[b, pl.ds(q * GROUP, GROUP)].reshape(WIDE, 256)
            e3 = dz[f, rows].reshape(WIDE, 256)
            d3 = e3 * a3 + c * slope_c + edge_rows(pat.at[f + 1], j)
            dz[f, rows] = d3.reshape(GROUP, WP, 256)
            return 0

        lax.fori_loop(0, frames * QUADS, to_d3, 0)

        def fill_back(side):
            present = lane > 0 if side == 0 else lane < lanes - 1
            f = -1 if side == 0 else frames

            @pl.when(present)
            def _():
                halo_wait(2 * b + 1, 2 + b, side)
                halo_wait(kind, b, side)

                def widen(j, _):
                    rows = pl.ds(j * GROUP, GROUP)
                    c = halo_recv[2 + b, side, rows].astype(F32).reshape(WIDE, 256)
                    e3 = halo_recv[b, side, rows].astype(F32).reshape(WIDE, 256)
                    d3 = e3 * a3 + c * slope_c + edge_rows(pat.at[f + 1], j)
                    hz[side, pl.ds(1 + j * GROUP, GROUP)] = d3.reshape(GROUP, WP, 256)
                    return 0

                lax.fori_loop(0, QUADS, widen, 0)

            @pl.when(jnp.logical_not(present))
            def _():
                def clear(j, _):
                    hz[side, pl.ds(1 + j * GROUP, GROUP)] = jnp.zeros((GROUP, WP, 256), F32)
                    return 0

                lax.fori_loop(0, QUADS, clear, 0)

        for side in range(2):
            fill_back(side)

        def emit_back(f):
            pad = pad_mask[:WP, :128] * live(f)

            def emit(row, half, cols, e2, carry):
                z = z2[b, f, row + 1, :, cols]
                d2 = (e2 * a2[:, cols] + (z * slope2[:, cols] + bias2[:, cols])) * pad
                d2s[f * HH + row, :, cols] = d2.astype(BF16)
                return carry

            return emit

        for f in range(frames):
            convolve(dz, f, b, True, emit_back(f), [])

        def unmixing(i, acc):
            _, lines, where = trio(i)
            e = dot(d2s[lines].reshape(TRIO * WIDE, 256), mix_t[b])
            z = z1[b, lines].reshape(TRIO * WIDE, 256)
            for k, (f, j) in enumerate(where):
                here = slice(WIDE * k, WIDE * (k + 1))
                v = z[here] * a1 + b1
                square, t = gelu_core(v)
                part = pl.ds((TRIO * i + k) * GROUP, GROUP)
                a1s[part] = gelu_value(v, t, half_mask(live(f), GROUP)).astype(BF16).reshape(GROUP, WP, 256)
                e1 = e[here] * gelu_slope(v, square, t, 0.5)
                conv[b, part] = e1.reshape(GROUP, WP, 256)
                acc = (acc[0] + fold(e1), acc[1] + fold(e1 * z[here]))
            return acc

        acc = lax.fori_loop(0, trios, unmixing, (zero8(), zero8()))
        if turn > 0:
            early[b + 1].finish(b + 1)
        total_start(base + 2, rows_of(*[flat_sum(a) for a in acc]))

        def depth_grad(half, b=b, a2=a2, b2=b2):
            place, at = (early[b], 80) if b == 0 else (final[b], 64)
            cols = slice(128 * half, 128 * (half + 1))
            taps_grad = tuple(zero8(128) for _ in range(KVOL))
            for f in range(frames):
                planes = []
                for dt in range(3):
                    g = f - (dt - 1)
                    planes.append(hz.at[0] if g < 0 else hz.at[1] if g > last else dz.at[g])
                shift_rows = b2[:, cols] * (pad_mask[:WP, :128] * live(f))

                def tap_rows(h, taps_grad):
                    a = z2[b, f, h + 1, :, cols] * a2[:, cols] + shift_rows
                    moved = [pltpu.roll(a, 1, 0), a, pltpu.roll(a, WP - 1, 0)]
                    new = list(taps_grad)
                    for dt in range(3):
                        for dh in range(3):
                            d = planes[dt][h + 1 - (dh - 1), :, cols]
                            for dw in range(3):
                                k = dt * 9 + dh * 3 + dw
                                new[k] = new[k] + fold(d * moved[dw])
                    return tuple(new)

                taps_grad = lax.fori_loop(0, HH, tap_rows, taps_grad)
            lines = jnp.concatenate(
                [flat_sum(t) for t in taps_grad] + [jnp.zeros((WP - KVOL, 128), F32)], axis=0
            )
            for r in range(4):
                part = jnp.concatenate([lines[8 * r : 8 * r + 8], zero8(128)], axis=0)
                for who in range(lanes):
                    place.put(who, 2 * r + half, at, part)

        depth_grad(0)
        if b == 0:
            depth_grad(1)
        g = dot_rows(d2s[...].reshape(frames * HH * WP, 256), a1s[...].reshape(frames * HH * WP, 256))
        for who in range(lanes):
            for r in range(4):
                for h in range(2):
                    first = share * who + 16 * r
                    early[b].put(who, 2 * r + h, 64, g[first : first + 16, 128 * h : 128 * (h + 1)])
        early[b].to_pair(b)

        got = total_finish(base + 2)
        slope1, bias1, gain1, shift1 = back_affine(got[0:1], got[1:2], count, norm1)
        mid_grads[b] = ((gain1, shift1), (gain2, shift2), (gain3, shift3))

        early[b].to_side(b)
        def first_grad(i):
            rows, lines, where = trio(i)
            e1 = conv[b, lines].reshape(TRIO * WIDE, 256)
            z = z1[b, lines].reshape(TRIO * WIDE, 256)
            parts = []
            for k, (f, j) in enumerate(where):
                here = slice(WIDE * k, WIDE * (k + 1))
                alive = live(f)
                parts.append(squeeze(e1[here] * a1 + (z[here] * (slope1 * alive) + bias1 * alive)))
            d1 = jnp.concatenate(parts, axis=0).astype(BF16)
            a3s[b, rows] = d1
            return rows, where, d1

        def reduce_grad(i, _):
            cols = pl.ds(pl.multiple_of(i * 256, 256), 256)
            g = dot_rows(a3s[b], xs[b][:, cols])
            for who in range(lanes):
                for h in range(2):
                    final[b].put(who, 2 * i + h, 0, g[share * who : share * (who + 1), 128 * h : 128 * (h + 1)])
            return 0

        if b > 0:

            def passing(i, carry):
                rows, where, d1 = first_grad(i)
                g = dot(d1, red_t[b]) + sb[rows].astype(F32)
                z, pre = open_block(b - 1, rows)
                s0, s1 = carry
                for k, (f, j) in enumerate(where):
                    here = slice(FLAT * k, FLAT * (k + 1))
                    v = pre[here]
                    square, t = gelu_core(v)
                    s = gelu_slope(v, square, t, 0.5 * live(f)) * g[here]
                    sb[pl.ds(pl.multiple_of((TRIO * i + k) * FLAT, FLAT), FLAT)] = s.astype(BF16)
                    s0, s1 = s0 + fold(s), s1 + fold(s * z[here])
                return s0, s1

            carry = lax.fori_loop(0, trios, passing, (zero8(1024), zero8(1024)))
            total_start(base + 3, rows_of(flat_sum(carry[0]), flat_sum(carry[1])))
            depth_grad(1)
            lax.fori_loop(0, 4, reduce_grad, 0)
            final[b].to_pair(b)
        else:
            final[b + 1].to_all(b + 1)

            def only_d1(i, _):
                first_grad(i)
                return 0

            lax.fori_loop(0, trios, only_d1, 0)
            final[b + 1].clear("a")
            lax.fori_loop(0, 4, reduce_grad, 0)
            final[b].to_pair(b)
            early[b + 1].clear("b", "all")
            early[b].to_rows(b)
            steps = (lambda: final[b].to_side(b), lambda: early[b].to_all(b))
            gtok_store = [frame_copy(yb, gtok_hbm, f, store_sem.at[f]) for f in range(frames)]
            for f in range(frames):
                rows = slice(f * frame_rows, (f + 1) * frame_rows)
                yb[rows] = (dot(a3s[b, rows], red_t[b]) + sb[rows].astype(F32)).astype(BF16)
                gtok_store[f].start()
                if f < len(steps):
                    steps[f]()
            final[b + 1].finish(b + 1)
            final[b + 1].clear("b", "all")
            final[b].to_rows(b)
            early[b].finish(b)
            final[b].to_all(b)
            final[b].finish(b)

    for b in range(BLOCKS):
        for k in range(3):
            for w in range(2):
                r = (b * 3 + k) * 2 + w
                gmid_out[r : r + 1] = mid_grads[b][k][w]
        for w in range(2):
            gout_out[2 * b + w : 2 * b + w + 1] = out_grads[b][w]

    for copy in gtok_store:
        copy.wait()
    early[0].clear("a", "b", "all")
    final[0].clear("a", "b", "all")
    for copy in late + travelling:
        copy.wait_send()
    for side in range(2):
        halo_sent(2 * BLOCKS + BLOCKS - 1, 0, side)


def whole_call(groups, lanes, counts, tokens, cotangent, reduce_loc, mix_loc, expand_loc, small_loc, norm_out):
    rows = tokens.shape[0]
    frames = rows // (HH * WW)
    whole = pl.BlockSpec(memory_space=pltpu.VMEM)
    hbm = pl.BlockSpec(memory_space=pl.ANY)
    dma = pltpu.SemaphoreType.DMA
    low, high = stages(groups)
    far = low * (lanes // 2)
    lines = frames * HH
    sums = 6 * BLOCKS
    kinds = 3 * BLOCKS
    shape = jax.ShapeDtypeStruct
    return pl.pallas_call(
        functools.partial(whole_kernel, groups, lanes),
        out_shape=(
            shape((rows, 1024), BF16),
            shape((rows, 1024), BF16),
            shape((BLOCKS, 176, 1024), F32),
            shape((BLOCKS * 6, 256), F32),
            shape((BLOCKS * 2, 1024), F32),
        ),
        in_specs=[pl.BlockSpec(memory_space=pltpu.SMEM)] + [hbm] * 5 + [whole] * 2,
        out_specs=[hbm] * 2 + [whole] * 3,
        scratch_shapes=[
            pltpu.VMEM((rows, 1024), BF16),
            pltpu.VMEM((rows, 1024), BF16),
            pltpu.VMEM((rows, 1024), BF16),
            pltpu.VMEM((rows, 1024), BF16),
            pltpu.VMEM((BLOCKS, 256, 1024), BF16),
            pltpu.VMEM((BLOCKS, 256, 1024), BF16),
            pltpu.VMEM((1024, 256), BF16),
            pltpu.VMEM((BLOCKS, 256, 256), BF16),
            pltpu.VMEM((256, 256), BF16),
            pltpu.VMEM((lanes,) + small_loc.shape, F32),
            pltpu.VMEM((2 * small_loc.shape[0], 256), F32),
            pltpu.VMEM((BLOCKS, lines, WP, 256), F32),
            pltpu.VMEM((lines, WP, 256), BF16),
            pltpu.VMEM((BLOCKS, frames, HH + 2, WP, 256), F32),
            pltpu.VMEM((frames, HH + 2, WP, 256), F32),
            pltpu.VMEM((2, HH + 2, WP, 256), F32),
            pltpu.VMEM((BLOCKS, lines, WP, 256), F32),
            pltpu.VMEM((BLOCKS, rows, 256), BF16),
            pltpu.VMEM((BLOCKS, frames + 2, 3, WP, 256), F32),
            pltpu.VMEM((frames + 2, 3, WP, 256), F32),
            pltpu.VMEM((lines, WP, 256), BF16),
            pltpu.VMEM((2, HH, WP, 256), BF16),
            pltpu.VMEM((2 * BLOCKS, 2, HH, WP, 256), BF16),
            pltpu.VMEM((lanes, PIECES, 176, 128), BF16),
            pltpu.VMEM((3, PIECES, 176, 128), BF16),
            pltpu.VMEM((PIECES, 176, 128), BF16),
            pltpu.VMEM((low, PIECES // low, 176, 128), BF16),
            pltpu.VMEM((PIECES, 176, 128), BF16),
            pltpu.VMEM((BLOCKS, high, PIECES // low, 176 if high > 1 else 16, 128), BF16),
            pltpu.VMEM((2, 2, 16, 128), F32),
            pltpu.VMEM((2, far, 16, 128), F32),
            pltpu.VMEM((2, high, 16, 128), F32),
            dma((sums,)),
            dma((sums,)),
            dma((sums, far)),
            dma((sums, far)),
            dma((sums, high)),
            dma((sums, high)),
            dma((7, 3)),
            dma((7, lanes)),
            dma((kinds, 2)),
            dma((kinds, 2)),
            dma((frames + 1,)),
            dma((frames,)),
            dma((2 * BLOCKS, 3)),
            dma((2 * BLOCKS, 3)),
            dma((2 * BLOCKS, low)),
            dma((2 * BLOCKS, low)),
            dma((2 * BLOCKS, low)),
            dma((2 * BLOCKS, low)),
            dma((2 * BLOCKS, high)),
            dma((2 * BLOCKS, high)),
            dma((BLOCKS, 4)),
        ],
        compiler_params=pltpu.CompilerParams(
            collective_id=1, has_side_effects=True, vmem_limit_bytes=63 * 2**20
        ),
    )(counts, tokens, cotangent, reduce_loc, mix_loc, expand_loc, small_loc, norm_out)


def descend(weight, moment, grad):
    moment_new = MOMENTUM * moment + grad + DECAY * weight
    return (weight - LEARN_RATE * moment_new, moment_new)


def update_kernel(lanes, *refs):
    out_raw, gtok_raw, reduced, gmid, gout = refs[:5]
    weights, moments = refs[5:11], refs[11:17]
    out, gtok = refs[17:19]
    grads, new_weights, new_moments = refs[19:25], refs[25:31], refs[31:37]
    held, sems, store_sems = refs[37:]
    rows = out.shape[0] // 3
    copies, stores = [], []
    for k in range(3):
        for which, (src, dst) in enumerate(((out_raw, out), (gtok_raw, gtok))):
            here = pl.ds(k * rows, rows)
            copies.append(pltpu.make_async_copy(src.at[here], held.at[which, here], sems.at[which, k]))
            stores.append(pltpu.make_async_copy(held.at[which, here], dst.at[here], store_sems.at[which, k]))
    for copy in copies:
        copy.start()
    lane = lax.axis_index("chan")
    narrow = 256 // lanes

    def mine(v):
        out = v[:, :narrow]
        for who in range(1, lanes):
            out = jnp.where(lane == who, v[:, narrow * who : narrow * (who + 1)], out)
        return out

    def step(slot, at, grad):
        weight, moment = descend(weights[slot][at], moments[slot][at], grad)
        grads[slot][at] = grad
        new_weights[slot][at] = weight
        new_moments[slot][at] = moment

    depths = []
    for b in range(BLOCKS):
        step(0, (b,), reduced[b, 96:160])
        mix = reduced[b, 64:80]
        step(1, (b,), jnp.concatenate([mix[:, 256 * r : 256 * (r + 1)] for r in range(4)], axis=0))
        depth = reduced[b, 80:88] if b == 0 else reduced[b, 160:168]
        depths.append(mine(jnp.concatenate([depth[:, 256 * r : 256 * (r + 1)] for r in range(4)], axis=0)))
        step(3, (b,), reduced[b, 0:64])
        step(5, (b,), gout[2 * b : 2 * b + 2])
    for k in range(KVOL):
        step(2, (k,), jnp.concatenate([depth[k : k + 1] for depth in depths], axis=0))
    middle = mine(gmid[...])
    for k in range(BLOCKS * 3):
        step(4, (k,), middle[2 * k : 2 * k + 2])
    for copy, store in zip(copies, stores):
        copy.wait()
        store.start()
    for store in stores:
        store.wait()


def update_call(lanes, *args):
    whole = pl.BlockSpec(memory_space=pltpu.VMEM)
    hbm = pl.BlockSpec(memory_space=pl.ANY)
    like = [jax.ShapeDtypeStruct(v.shape, v.dtype) for v in args]
    return pl.pallas_call(
        functools.partial(update_kernel, lanes),
        out_shape=tuple(like[:2] + like[5:11] * 3),
        in_specs=[hbm] * 2 + [whole] * 15,
        out_specs=[hbm] * 2 + [whole] * 18,
        scratch_shapes=[
            pltpu.VMEM((2,) + args[0].shape, args[0].dtype),
            pltpu.SemaphoreType.DMA((2, 3)),
            pltpu.SemaphoreType.DMA((2, 3)),
        ],
        compiler_params=pltpu.CompilerParams(vmem_limit_bytes=60 * 2**20),
    )(*args)


def shards(
    tokens,
    frame_counts,
    cotangent,
    w_reduce,
    w_mix,
    w_depth,
    w_expand,
    norm_mid,
    norm_out,
    moment_reduce,
    moment_mix,
    moment_depth,
    moment_expand,
    moment_mid,
    moment_out,
):
    lane = lax.axis_index("chan")
    lanes = lax.axis_size("chan")
    narrow = w_reduce.shape[2]
    small = jnp.concatenate([w_depth.reshape(-1, narrow), norm_mid.reshape(-1, narrow)], axis=0)
    small = jnp.pad(small, ((0, -small.shape[0] % 16), (0, 0)))
    small = jnp.concatenate(jnp.split(small, 2, axis=0), axis=1)
    turned = lambda v: jnp.swapaxes(v, 1, 2)
    raw = whole_call(
        lax.axis_size("dp"),
        lanes,
        frame_counts,
        tokens,
        cotangent,
        turned(w_reduce),
        turned(w_mix),
        w_expand,
        small,
        norm_out,
    )
    swap = lambda v: jnp.swapaxes(v, 0, 1)
    flat = lambda v: v.reshape((-1,) + v.shape[2:])
    inside = lambda r, m, d, e, mid, out: (turned(r), turned(m), swap(d), e, flat(mid), out)
    outside = lambda r, m, d, e, mid, out: (turned(r), turned(m), swap(d), e, mid.reshape(norm_mid.shape), out)
    done = update_call(
        lanes,
        *raw,
        *inside(w_reduce, w_mix, w_depth, w_expand, norm_mid, norm_out),
        *inside(moment_reduce, moment_mix, moment_depth, moment_expand, moment_mid, moment_out),
    )
    return done[:2] + outside(*done[2:8]) + outside(*done[8:14]) + outside(*done[14:20])


def solution(mesh):
    rows = P(("dp", "chan"), None)
    weights = (
        P(None, None, "chan"),
        P(None, None, "chan"),
        P(None, None, "chan"),
        P(None, "chan", None),
        P(None, None, None, "chan"),
        P(),
    )
    return jax.shard_map(
        shards,
        mesh=mesh,
        in_specs=(rows, P("dp"), rows) + weights + weights,
        out_specs=(rows, rows) + weights + weights + weights,
        check_vma=False,
    )
```

profile of v0, /device:TPU:0, one launch (start us, length us, event | category | flops | bytes accessed | tf_op | source)
XLA Modules:
  0.0 235.8 jit_solution(17801065171933148555)
XLA Ops:
  1.3 0.7 reshape.62
  2.0 0.7 copy.36
  2.8 0.7 pad_maximum_fusion.small_loc
  3.5 220.7 %shard_map.302 = (bf16[2352,1024]{1,0:T(8,128)(2,1)}, bf16[2352,1024]{1,0:T(8,128)(2,1)}, f32[2,176,1024]{2,1,0:T(8,128)}, f32[12,256]{1,0:T(8,128)}, f32[4,1024]{1,0:T(4,128)}) custom-call(s32[1]{0:T(128)S(6)} %copy.37.counts, bf16[2352,1024]{1,0:T(8,128)(2,1)} %tokens.1, bf16[2352,1024]{1,0:T(8,128)(2,1)} %cotangent.1, f32[2,64,1024]{2,1,0:T(8,128)} %bitcast.20, ...), custom_call_target="tpu_custom_call" | custom-call | tf_op jit(solution)/shard_map/pallas_call | solution.py:1154
  224.1 11.4 %shard_map.303 = (bf16[2352,1024]{1,0:T(8,128)(2,1)}, bf16[2352,1024]{1,0:T(8,128)(2,1)}, f32[2,64,1024]{2,1,0:T(8,128)}, f32[2,64,256]{2,1,0:T(8,128)}, f32[27,...) custom-call(bf16[2352,1024]{1,0:T(8,128)(2,1)} %get-tuple-element.45, ...), custom_call_target="tpu_custom_call" | custom-call | tf_op jit(solution)/shard_map/pallas_call | solution.py:1286
  (2 shorter events, 0.0 us)
where the time goes:
time: 236 us
  Pallas kernels  232 us (98%)
    pallas_call x1, Pallas kernels, whole_call(): pl.pallas_call(functools.partial(whole_kernel, groups, lanes), out_shape=...  221 us
    pallas_call x1, Pallas kernels, update_call(): pl.pallas_call(functools.partial(update_kernel, lanes), out_shape=tuple(l...  11.4 us

commit v1 on v0

--- a/solution.py
+++ b/solution.py
@@ -171,6 +171,8 @@
     grads_out,
     gmid_out,
     gout_out,
+    keep_big,
+    keep_mid,
     x0,
     x1,
     yb,
@@ -192,6 +194,7 @@
     edge,
     pat,
     d2s,
+    d1s,
     halo_send,
     halo_recv,
     grad_a,
@@ -224,6 +227,8 @@
     grad_st,
     grad_qt,
     weight_sem,
+    keep_sem,
+    back_sem,
 ):
     net = Net(groups, lanes)
     lane = net.lane
@@ -677,6 +682,20 @@
         a4, b4 = norms[b][3][2], norms[b][3][3]
         return z, (z * a4 + b4) + xs[b][rows].astype(F32)
 
+    kept = [(a1s, keep_mid.at[0]), (d1s, keep_mid.at[1]), (d2s, keep_mid.at[2]), (yb, keep_big)]
+    keeps = [pltpu.make_async_copy(held, far_away, keep_sem.at[k]) for k, (held, far_away) in enumerate(kept)]
+    backs = [pltpu.make_async_copy(far_away, held, back_sem.at[k]) for k, (held, far_away) in enumerate(kept)]
+
+    def slope_rows(i, _):
+        rows, lines, where = trio(i)
+        _, pre = open_block(0, rows)
+        for k, (f, j) in enumerate(where):
+            v = pre[FLAT * k : FLAT * (k + 1)]
+            square, t = gelu_core(v)
+            part = pl.ds(pl.multiple_of((TRIO * i + k) * FLAT, FLAT), FLAT)
+            yb[part] = gelu_slope(v, square, t, 0.5 * live(f)).astype(BF16)
+        return 0
+
     out_store = [frame_copy(yb, out_hbm, f, store_sem.at[f]) for f in range(frames)]
 
     for b in range(BLOCKS):
@@ -686,6 +705,7 @@
         _, _, a1, b1 = norm1
         carry = (zero8(), zero8())
         if b > 0:
+            keeps[0].wait()
             for side in range(2):
                 halo_sent(2 * (b - 1) + 1, 2 + b - 1, side)
         for f in order:
@@ -693,13 +713,18 @@
 
             v = z1[b, f * HH : (f + 1) * HH].reshape(HH * WP, 256) * a1 + b1
             _, t = gelu_core(v)
-            m = dot(gelu_value(v, t, half_mask(alive, HH)).astype(BF16), mix[...])
+            act = gelu_value(v, t, half_mask(alive, HH)).astype(BF16)
+            a1s[f * HH : (f + 1) * HH] = act.reshape(HH, WP, 256)
+            m = dot(act, mix[...])
             z2[b, f, 1 : 1 + HH] = m.reshape(HH, WP, 256)
             if f in (0, last):
                 halo_send[0 if f == 0 else 1] = m.astype(BF16).reshape(HH, WP, 256)
             carry = (carry[0] + fold(m), carry[1] + fold(m * m))
             if f in (0, last):
                 halo_start(2 * b, b, 0 if f == 0 else 1)
+
+        if b == 0:
+            keeps[0].start()
 
         def emit_conv(f):
             pad = pad_mask[:WP, :128] * live(f)
@@ -754,6 +779,21 @@
         else:
             gather_wait("exp", 1)
             tbuf[...] = exp[1].T
+            keeps[1].wait()
+
+        def slope1(i, _):
+            _, lines, where = trio(i)
+            v = z1[b, lines].reshape(TRIO * WIDE, 256) * a1 + b1
+            square, t = gelu_core(v)
+            d1s[lines] = gelu_slope(v, square, t, 0.5).astype(BF16).reshape(TRIO * GROUP, WP, 256)
+            return 0
+
+        lax.fori_loop(0, trios, slope1, 0)
+        if b == 0:
+            keeps[1].start()
+        else:
+            lax.fori_loop(trios - 2, trios, slope_rows, 0)
+            keeps[3].start()
         got = total_finish(3 * b + 1)
         norm2 = affine(got[0:1], got[1:2], count, mid(b, 1, 0), mid(b, 1, 1))
         _, _, a2, b2 = norm2
@@ -793,6 +833,23 @@
         if b == 0:
             gather_wait("red", 1)
             tbuf[...] = red_t[1].T
+        else:
+            keeps[2].wait()
+
+        def slope3(i, _):
+            _, lines, where = trio(i)
+            c = conv[b, lines].reshape(TRIO * WIDE, 256)
+            out = []
+            for k, (f, j) in enumerate(where):
+                v = c[WIDE * k : WIDE * (k + 1)] * (a3 * a2) + edge_rows(pat.at[f + 1], j)
+                square, t = gelu_core(v)
+                out.append(gelu_slope(v, square, t, 0.5).astype(BF16))
+            d2s[lines] = jnp.concatenate(out, axis=0).reshape(TRIO * GROUP, WP, 256)
+            return 0
+
+        lax.fori_loop(0, trios, slope3, 0)
+        if b == 0:
+            keeps[2].start()
         got = total_finish(3 * b + 2)
         norm4 = affine(wide_row(got, 0), wide_row(got, 4), count4, norm_out[b, 0:1], norm_out[b, 1:2])
         norms.append((norm1, norm2, norm3, norm4, (sc, scc, sce, se, see)))
@@ -818,10 +875,12 @@
             total_start(3, rows_of(flat_sum(carry[0]), flat_sum(carry[1])))
             gather_wait("mix", 1)
             mix[...] = mix_t[1].T
+            lax.fori_loop(0, trios - 2, slope_rows, 0)
             got = total_finish(3)
             first_sums = (got[0:1], got[1:2])
 
     cot_load.wait()
+    keeps[3].wait()
 
     def ending(i, carry):
         rows, lines, where = trio(i)
@@ -869,7 +928,8 @@
             early[b + 1].to_rows(b + 1)
             final[b + 1].to_side(b + 1)
         kind = 2 * BLOCKS + turn
-        norm3_pattern(b, a3, b2, b3)
+        if turn > 0:
+            backs[2].wait()
         acc = (zero8(), zero8(), zero8())
         for f in order:
             alive = live(f)
@@ -881,9 +941,8 @@
             back = spread(dot(d4, tbuf[...]))
             for j in range(QUADS):
                 c = conv[b, f * HH + GROUP * j : f * HH + GROUP * (j + 1)].reshape(WIDE, 256)
-                v = c * (a3 * a2) + edge_rows(pat.at[f + 1], j)
-                square, t = gelu_core(v)
-                e3 = back[WIDE * j : WIDE * (j + 1)] * gelu_slope(v, square, t, 0.5)
+                slope = d2s[f * HH + GROUP * j : f * HH + GROUP * (j + 1)].reshape(WIDE, 256)
+                e3 = back[WIDE * j : WIDE * (j + 1)] * slope.astype(F32)
                 dz[f, 1 + GROUP * j : 1 + GROUP * (j + 1)] = e3.reshape(GROUP, WP, 256)
                 if f in (0, last):
                     halo_send[0 if f == 0 else 1, GROUP * j : GROUP * (j + 1)] = e3.astype(BF16).reshape(GROUP, WP, 256)
@@ -907,6 +966,7 @@
         lax.fori_loop(0, 4, expand_grad, 0)
         if b > 0:
             tbuf[...] = exp[b - 1].T
+            backs[3].start()
 
         got = total_finish(base + 1)
         e3_sum, e3_conv, e3_edge = got[0:1], got[1:2], got[2:3]
@@ -983,17 +1043,18 @@
         for f in range(frames):
             convolve(dz, f, b, True, emit_back(f), [])
 
+        if turn > 0:
+            backs[0].wait()
+            backs[1].wait()
+
         def unmixing(i, acc):
             _, lines, where = trio(i)
             e = dot(d2s[lines].reshape(TRIO * WIDE, 256), mix_t[b])
             z = z1[b, lines].reshape(TRIO * WIDE, 256)
             for k, (f, j) in enumerate(where):
                 here = slice(WIDE * k, WIDE * (k + 1))
-                v = z[here] * a1 + b1
-                square, t = gelu_core(v)
                 part = pl.ds((TRIO * i + k) * GROUP, GROUP)
-                a1s[part] = gelu_value(v, t, half_mask(live(f), GROUP)).astype(BF16).reshape(GROUP, WP, 256)
-                e1 = e[here] * gelu_slope(v, square, t, 0.5)
+                e1 = e[here] * d1s[part].reshape(WIDE, 256).astype(F32)
                 conv[b, part] = e1.reshape(GROUP, WP, 256)
                 acc = (acc[0] + fold(e1), acc[1] + fold(e1 * z[here]))
             return acc
@@ -1045,6 +1106,9 @@
                     first = share * who + 16 * r
                     early[b].put(who, 2 * r + h, 64, g[first : first + 16, 128 * h : 128 * (h + 1)])
         early[b].to_pair(b)
+        if b > 0:
+            for k in range(3):
+                backs[k].start()
 
         got = total_finish(base + 2)
         slope1, bias1, gain1, shift1 = back_affine(got[0:1], got[1:2], count, norm1)
@@ -1074,16 +1138,17 @@
 
         if b > 0:
 
+            backs[3].wait()
+
             def passing(i, carry):
                 rows, where, d1 = first_grad(i)
                 g = dot(d1, red_t[b]) + sb[rows].astype(F32)
-                z, pre = open_block(b - 1, rows)
+                z = dot(a3s[b - 1, rows], exp[b - 1])
+                slope = yb[rows]
                 s0, s1 = carry
                 for k, (f, j) in enumerate(where):
                     here = slice(FLAT * k, FLAT * (k + 1))
-                    v = pre[here]
-                    square, t = gelu_core(v)
-                    s = gelu_slope(v, square, t, 0.5 * live(f)) * g[here]
+                    s = slope[here].astype(F32) * g[here]
                     sb[pl.ds(pl.multiple_of((TRIO * i + k) * FLAT, FLAT), FLAT)] = s.astype(BF16)
                     s0, s1 = s0 + fold(s), s1 + fold(s * z[here])
                 return s0, s1
@@ -1159,9 +1224,11 @@
             shape((BLOCKS, 176, 1024), F32),
             shape((BLOCKS * 6, 256), F32),
             shape((BLOCKS * 2, 1024), F32),
+            shape((rows, 1024), BF16),
+            shape((3, lines, WP, 256), BF16),
         ),
         in_specs=[pl.BlockSpec(memory_space=pltpu.SMEM)] + [hbm] * 5 + [whole] * 2,
-        out_specs=[hbm] * 2 + [whole] * 3,
+        out_specs=[hbm] * 2 + [whole] * 3 + [hbm] * 2,
         scratch_shapes=[
             pltpu.VMEM((rows, 1024), BF16),
             pltpu.VMEM((rows, 1024), BF16),
@@ -1183,6 +1250,7 @@
             pltpu.VMEM((BLOCKS, rows, 256), BF16),
             pltpu.VMEM((BLOCKS, frames + 2, 3, WP, 256), F32),
             pltpu.VMEM((frames + 2, 3, WP, 256), F32),
+            pltpu.VMEM((lines, WP, 256), BF16),
             pltpu.VMEM((lines, WP, 256), BF16),
             pltpu.VMEM((2, HH, WP, 256), BF16),
             pltpu.VMEM((2 * BLOCKS, 2, HH, WP, 256), BF16),
@@ -1216,6 +1284,8 @@
             dma((2 * BLOCKS, high)),
             dma((2 * BLOCKS, high)),
             dma((BLOCKS, 4)),
+            dma((4,)),
+            dma((4,)),
         ],
         compiler_params=pltpu.CompilerParams(
             collective_id=1, has_side_effects=True, vmem_limit_bytes=63 * 2**20
@@ -1229,20 +1299,27 @@
 
 
 def update_kernel(lanes, *refs):
-    out_raw, gtok_raw, reduced, gmid, gout = refs[:5]
-    weights, moments = refs[5:11], refs[11:17]
+    out_raw, gtok_raw = refs[:2]
     out, gtok = refs[17:19]
-    grads, new_weights, new_moments = refs[19:25], refs[25:31], refs[31:37]
-    held, sems, store_sems = refs[37:]
-    rows = out.shape[0] // 3
+    held = refs[37:70]
+    big, sems, store_sems, small_sems, small_stores = refs[70:]
+    smalls = [pltpu.make_async_copy(refs[2 + k], held[k], small_sems.at[k]) for k in range(15)]
+    results = [pltpu.make_async_copy(held[15 + k], refs[19 + k], small_stores.at[k]) for k in range(18)]
+    reduced, gmid, gout = held[:3]
+    weights, moments = held[3:9], held[9:15]
+    grads, new_weights, new_moments = held[15:21], held[21:27], held[27:33]
+    chunks = sems.shape[1]
+    rows = out.shape[0] // chunks
     copies, stores = [], []
-    for k in range(3):
+    for k in range(chunks):
         for which, (src, dst) in enumerate(((out_raw, out), (gtok_raw, gtok))):
             here = pl.ds(k * rows, rows)
-            copies.append(pltpu.make_async_copy(src.at[here], held.at[which, here], sems.at[which, k]))
-            stores.append(pltpu.make_async_copy(held.at[which, here], dst.at[here], store_sems.at[which, k]))
-    for copy in copies:
+            copies.append(pltpu.make_async_copy(src.at[here], big.at[which, here], sems.at[which, k]))
+            stores.append(pltpu.make_async_copy(big.at[which, here], dst.at[here], store_sems.at[which, k]))
+    for copy in smalls + copies:
         copy.start()
+    for copy in smalls:
+        copy.wait()
     lane = lax.axis_index("chan")
     narrow = 256 // lanes
 
@@ -1272,26 +1349,30 @@
     middle = mine(gmid[...])
     for k in range(BLOCKS * 3):
         step(4, (k,), middle[2 * k : 2 * k + 2])
+    for copy in results:
+        copy.start()
     for copy, store in zip(copies, stores):
         copy.wait()
         store.start()
-    for store in stores:
+    for store in stores + results:
         store.wait()
 
 
 def update_call(lanes, *args):
-    whole = pl.BlockSpec(memory_space=pltpu.VMEM)
     hbm = pl.BlockSpec(memory_space=pl.ANY)
     like = [jax.ShapeDtypeStruct(v.shape, v.dtype) for v in args]
     return pl.pallas_call(
         functools.partial(update_kernel, lanes),
         out_shape=tuple(like[:2] + like[5:11] * 3),
-        in_specs=[hbm] * 2 + [whole] * 15,
-        out_specs=[hbm] * 2 + [whole] * 18,
-        scratch_shapes=[
+        in_specs=[hbm] * 17,
+        out_specs=[hbm] * 20,
+        scratch_shapes=[pltpu.VMEM(v.shape, v.dtype) for v in like[2:] + like[5:11] * 3]
+        + [
             pltpu.VMEM((2,) + args[0].shape, args[0].dtype),
-            pltpu.SemaphoreType.DMA((2, 3)),
-            pltpu.SemaphoreType.DMA((2, 3)),
+            pltpu.SemaphoreType.DMA((2, 7)),
+            pltpu.SemaphoreType.DMA((2, 7)),
+            pltpu.SemaphoreType.DMA((15,)),
+            pltpu.SemaphoreType.DMA((18,)),
         ],
         compiler_params=pltpu.CompilerParams(vmem_limit_bytes=60 * 2**20),
     )(*args)
@@ -1339,7 +1420,7 @@
     outside = lambda r, m, d, e, mid, out: (turned(r), turned(m), swap(d), e, mid.reshape(norm_mid.shape), out)
     done = update_call(
         lanes,
-        *raw,
+        *raw[:5],
         *inside(w_reduce, w_mix, w_depth, w_expand, norm_mid, norm_out),
         *inside(moment_reduce, moment_mix, moment_depth, moment_expand, moment_mid, moment_out),
     )

time: 236 us -> 227 us (0.962)
  Pallas kernels: 232 us -> 223 us
    pallas_call x1, Pallas kernels: 221 us -> 213 us  [whole_call(): pl.pallas_call(functools.partial(whole_kernel, groups, lanes), out_shape=...]
where the time goes in v1:
time: 227 us
  Pallas kernels  223 us (98%)
    pallas_call x1, Pallas kernels, whole_call(): pl.pallas_call(functools.partial(whole_kernel, groups, lanes), out_shape=...  213 us
    pallas_call x1, Pallas kernels, update_call(): pl.pallas_call(functools.partial(update_kernel, lanes), out_shape=tuple(l...  10.5 us

profile of v1, /device:TPU:0, one launch (start us, length us, event | category | flops | bytes accessed | tf_op | source)
XLA Modules:
  0.0 226.8 jit_solution(10446618392666286962)
XLA Ops:
  1.3 0.7 reshape.62
  2.0 0.7 copy.36
  2.8 0.7 pad_maximum_fusion.small_loc
  3.5 212.6 %shard_map.302 = (bf16[2352,1024]{1,0:T(8,128)(2,1)}, bf16[2352,1024]{1,0:T(8,128)(2,1)}, f32[2,176,1024]{2,1,0:T(8,128)}, f32[12,256]{1,0:T(8,128)}, f32[4,1024...) custom-call(s32[1]{0:T(128)S(6)} %copy.37.counts, bf16[2352,1024]{1,0:T(8,128)(2,1)} %tokens.1, ...), custom_call_target="tpu_custom_call" | custom-call | tf_op jit(solution)/shard_map/pallas_call | solution.py:1219
  216.1 10.5 %shard_map.303 = (bf16[2352,1024]{1,0:T(8,128)(2,1)}, bf16[2352,1024]{1,0:T(8,128)(2,1)}, f32[2,64,1024]{2,1,0:T(8,128)}, f32[2,64,256]{2,1,0:T(8,128)}, f32[27,...) custom-call(bf16[2352,1024]{1,0:T(8,128)(2,1)} %get-tuple-element.45, ...), custom_call_target="tpu_custom_call" | custom-call | tf_op jit(solution)/shard_map/pallas_call | solution.py:1364
  (2 shorter events, 0.0 us)

commit v2 on v1

--- a/solution.py
+++ b/solution.py
@@ -164,7 +164,8 @@
     reduce_loc,
     mix_loc,
     expand_loc,
-    small_loc,
+    depth_loc,
+    mid_loc,
     norm_out,
     out_hbm,
     gtok_hbm,
@@ -287,7 +288,12 @@
             parts = [grads_out[b, 128:160, :256], grads_out[b, 128:160, 256:512]]
             mine[...] = jnp.concatenate(parts, axis=0).astype(BF16)
         else:
-            mine[...] = small_loc[...]
+            half_rows = small.shape[0] // 2
+            lines = [depth_loc[k, b : b + 1] for b in range(BLOCKS) for k in range(KVOL)]
+            lines += [mid_loc[k, w : w + 1] for k in range(3 * BLOCKS) for w in range(2)]
+            for r, line in enumerate(lines):
+                side = r // half_rows
+                mine[r - side * half_rows : r - side * half_rows + 1, 64 * side : 64 * (side + 1)] = line
         for step, (_, device) in enumerate((net.pair(), net.across())):
             copy = push(mine, mine, gather_send.at[slot, step], gather_recv.at[slot, own], device)
             copy.start()
@@ -455,7 +461,7 @@
     total_start(0, rows_of(flat_sum(carry[0]), flat_sum(carry[1]), here_count))
 
     gather_wait("small", 0)
-    half_rows = small_loc.shape[0]
+    half_rows = small.shape[0] // 2
     for side in range(2):
         here = [small_in[who, :, 64 * side : 64 * (side + 1)] for who in range(lanes)]
         small[half_rows * side : half_rows * (side + 1)] = jnp.concatenate(here, axis=1)
@@ -619,17 +625,19 @@
             self.across_copy(b).wait_recv()
             self.clear("b")
 
-            def add(piece, _):
+            def add(piece):
                 total = grad_a[own, piece, self.lines].astype(F32) + grad_ra[net.side, piece, self.lines].astype(F32)
                 grad_b[piece, self.lines] = (total + grad_ra[2, piece, self.lines].astype(F32)).astype(BF16)
-                return 0
-
-            lax.fori_loop(0, PIECES, add, 0)
+
             each = PIECES // net.low
             for step, (who, device) in enumerate(self.low_peers()):
+                for k in range(each):
+                    add(who * each + k)
                 src = grad_b.at[pl.ds(who * each, each), self.lines]
                 dst = grad_rb.at[net.row_low, :, self.lines]
                 self.move("b", push(src, dst, grad_sb.at[i, step], grad_qb.at[i, net.row_low], device))
+            for k in range(each):
+                add(net.row_low * each + k)
 
         def to_all(self, b):
             i = 2 * b + self.which
@@ -862,8 +870,10 @@
                 _, pre = open_block(0, rows)
                 results = []
                 for (f, j), v in zip(where, pieces(pre, FLAT)):
+                    half = jnp.full((1, 1024), 0.5 * live(f), F32).astype(BF16)
+                    v = v.astype(BF16)
                     _, t = gelu_core(v)
-                    results.append(gelu_value(v, t, 0.5 * live(f)).astype(BF16))
+                    results.append(gelu_value(v, t, half))
                 result = jnp.concatenate(results, axis=0)
                 x1[rows] = result
                 z = dot(result, tbuf[...])
@@ -889,12 +899,13 @@
         s0, s1 = carry
         for k, (f, j) in enumerate(where):
             here = slice(FLAT * k, FLAT * (k + 1))
-            v, half = pre[here], 0.5 * live(f)
+            v, half = pre[here].astype(BF16), jnp.full((1, 1024), 0.5 * live(f), F32).astype(BF16)
             square, t = gelu_core(v)
             part = pl.ds(pl.multiple_of((TRIO * i + k) * FLAT, FLAT), FLAT)
-            yb[part] = gelu_value(v, t, half).astype(BF16)
-            s = gelu_slope(v, square, t, half) * g[here].astype(F32)
-            sb[part] = s.astype(BF16)
+            yb[part] = gelu_value(v, t, half)
+            low = gelu_slope(v, square, t, half) * g[here]
+            sb[part] = low
+            s = low.astype(F32)
             s0, s1 = s0 + fold(s), s1 + fold(s * z[here])
         return s0, s1
 
@@ -1204,7 +1215,7 @@
         halo_sent(2 * BLOCKS + BLOCKS - 1, 0, side)
 
 
-def whole_call(groups, lanes, counts, tokens, cotangent, reduce_loc, mix_loc, expand_loc, small_loc, norm_out):
+def whole_call(groups, lanes, counts, tokens, cotangent, reduce_loc, mix_loc, expand_loc, depth_loc, mid_loc, norm_out):
     rows = tokens.shape[0]
     frames = rows // (HH * WW)
     whole = pl.BlockSpec(memory_space=pltpu.VMEM)
@@ -1227,7 +1238,7 @@
             shape((rows, 1024), BF16),
             shape((3, lines, WP, 256), BF16),
         ),
-        in_specs=[pl.BlockSpec(memory_space=pltpu.SMEM)] + [hbm] * 5 + [whole] * 2,
+        in_specs=[pl.BlockSpec(memory_space=pltpu.SMEM)] + [hbm] * 5 + [whole] * 3,
         out_specs=[hbm] * 2 + [whole] * 3 + [hbm] * 2,
         scratch_shapes=[
             pltpu.VMEM((rows, 1024), BF16),
@@ -1239,8 +1250,8 @@
             pltpu.VMEM((1024, 256), BF16),
             pltpu.VMEM((BLOCKS, 256, 256), BF16),
             pltpu.VMEM((256, 256), BF16),
-            pltpu.VMEM((lanes,) + small_loc.shape, F32),
-            pltpu.VMEM((2 * small_loc.shape[0], 256), F32),
+            pltpu.VMEM((lanes, 40, 128), F32),
+            pltpu.VMEM((80, 256), F32),
             pltpu.VMEM((BLOCKS, lines, WP, 256), F32),
             pltpu.VMEM((lines, WP, 256), BF16),
             pltpu.VMEM((BLOCKS, frames, HH + 2, WP, 256), F32),
@@ -1290,7 +1301,7 @@
         compiler_params=pltpu.CompilerParams(
             collective_id=1, has_side_effects=True, vmem_limit_bytes=63 * 2**20
         ),
-    )(counts, tokens, cotangent, reduce_loc, mix_loc, expand_loc, small_loc, norm_out)
+    )(counts, tokens, cotangent, reduce_loc, mix_loc, expand_loc, depth_loc, mid_loc, norm_out)
 
 
 def descend(weight, moment, grad):
@@ -1395,13 +1406,10 @@
     moment_mid,
     moment_out,
 ):
-    lane = lax.axis_index("chan")
     lanes = lax.axis_size("chan")
-    narrow = w_reduce.shape[2]
-    small = jnp.concatenate([w_depth.reshape(-1, narrow), norm_mid.reshape(-1, narrow)], axis=0)
-    small = jnp.pad(small, ((0, -small.shape[0] % 16), (0, 0)))
-    small = jnp.concatenate(jnp.split(small, 2, axis=0), axis=1)
     turned = lambda v: jnp.swapaxes(v, 1, 2)
+    swap = lambda v: jnp.swapaxes(v, 0, 1)
+    flat = lambda v: v.reshape((-1,) + v.shape[2:])
     raw = whole_call(
         lax.axis_size("dp"),
         lanes,
@@ -1411,11 +1419,10 @@
         turned(w_reduce),
         turned(w_mix),
         w_expand,
-        small,
+        swap(w_depth),
+        flat(norm_mid),
         norm_out,
     )
-    swap = lambda v: jnp.swapaxes(v, 0, 1)
-    flat = lambda v: v.reshape((-1,) + v.shape[2:])
     inside = lambda r, m, d, e, mid, out: (turned(r), turned(m), swap(d), e, flat(mid), out)
     outside = lambda r, m, d, e, mid, out: (turned(r), turned(m), swap(d), e, mid.reshape(norm_mid.shape), out)
     done = update_call(

time: 227 us -> 221 us (0.974)
  Pallas kernels: 223 us -> 219 us
    pallas_call x1, Pallas kernels: 213 us -> 209 us  [whole_call(): pl.pallas_call(functools.partial(whole_kernel, groups, lanes), out_shape=...]
where the time goes in v2:
time: 221 us
  Pallas kernels  219 us (99%)
    pallas_call x1, Pallas kernels, whole_call(): pl.pallas_call(functools.partial(whole_kernel, groups, lanes), out_shape=...  209 us
    pallas_call x1, Pallas kernels, update_call(): pl.pallas_call(functools.partial(update_kernel, lanes), out_shape=tuple(l...  10.5 us

profile of v2, /device:TPU:0, one launch (start us, length us, event | category | flops | bytes accessed | tf_op | source)
XLA Modules:
  0.0 220.8 jit_solution(16796518573228591583)
XLA Ops:
  1.3 208.8 %shard_map.302 = (bf16[2352,1024]{1,0:T(8,128)(2,1)}, bf16[2352,1024]{1,0:T(8,128)(2,1)}, f32[2,176,1024]{2,1,0:T(8,128)}, f32[12,256]{1,0:T(8,128)}, f32[4,1024...) custom-call(s32[1]{0:T(128)S(6)} %copy.35.counts, bf16[2352,1024]{1,0:T(8,128)(2,1)} %tokens.1, ...), custom_call_target="tpu_custom_call" | custom-call | tf_op jit(solution)/shard_map/pallas_call | solution.py:1230
  210.1 10.5 %shard_map.303 = (bf16[2352,1024]{1,0:T(8,128)(2,1)}, bf16[2352,1024]{1,0:T(8,128)(2,1)}, f32[2,64,1024]{2,1,0:T(8,128)}, f32[2,64,256]{2,1,0:T(8,128)}, f32[27,...) custom-call(bf16[2352,1024]{1,0:T(8,128)(2,1)} %get-tuple-element.45, ...), custom_call_target="tpu_custom_call" | custom-call | tf_op jit(solution)/shard_map/pallas_call | solution.py:1375

commit v3 on v2

--- a/solution.py
+++ b/solution.py
@@ -719,9 +719,9 @@
         for f in order:
             alive = live(f)
 
-            v = z1[b, f * HH : (f + 1) * HH].reshape(HH * WP, 256) * a1 + b1
+            v = (z1[b, f * HH : (f + 1) * HH].reshape(HH * WP, 256) * a1 + b1).astype(BF16)
             _, t = gelu_core(v)
-            act = gelu_value(v, t, half_mask(alive, HH)).astype(BF16)
+            act = gelu_value(v, t, half_mask(alive, HH).astype(BF16))
             a1s[f * HH : (f + 1) * HH] = act.reshape(HH, WP, 256)
             m = dot(act, mix[...])
             z2[b, f, 1 : 1 + HH] = m.reshape(HH, WP, 256)

time: 221 us -> 221 us (level)
  no operation moved by 1% of the time
where the time goes in v3:
time: 221 us
  Pallas kernels  219 us (99%)
    pallas_call x1, Pallas kernels, whole_call(): pl.pallas_call(functools.partial(whole_kernel, groups, lanes), out_shape=...  209 us
    pallas_call x1, Pallas kernels, update_call(): pl.pallas_call(functools.partial(update_kernel, lanes), out_shape=tuple(l...  10.5 us

profile of v3, /device:TPU:0, one launch (start us, length us, event | category | flops | bytes accessed | tf_op | source)
XLA Modules:
  0.0 220.6 jit_solution(14127824357665699068)
XLA Ops:
  1.3 208.6 %shard_map.302 = (bf16[2352,1024]{1,0:T(8,128)(2,1)}, bf16[2352,1024]{1,0:T(8,128)(2,1)}, f32[2,176,1024]{2,1,0:T(8,128)}, f32[12,256]{1,0:T(8,128)}, f32[4,1024...) custom-call(s32[1]{0:T(128)S(6)} %copy.35.counts, bf16[2352,1024]{1,0:T(8,128)(2,1)} %tokens.1, ...), custom_call_target="tpu_custom_call" | custom-call | tf_op jit(solution)/shard_map/pallas_call | solution.py:1230
  209.9 10.5 %shard_map.303 = (bf16[2352,1024]{1,0:T(8,128)(2,1)}, bf16[2352,1024]{1,0:T(8,128)(2,1)}, f32[2,64,1024]{2,1,0:T(8,128)}, f32[2,64,256]{2,1,0:T(8,128)}, f32[27,...) custom-call(bf16[2352,1024]{1,0:T(8,128)(2,1)} %get-tuple-element.45, ...), custom_call_target="tpu_custom_call" | custom-call | tf_op jit(solution)/shard_map/pallas_call | solution.py:1375
